TPU v7x, 32 devices: a whole 2x2x4 slice. The times are simulated.
32 devices in a mesh: ctx: 4 (over y, x), ch: 8 (over z, core).
Axes of the slice: x: 2, y: 2, z: 4, core: 2. Of those that a mesh axis runs over, the one named last changes fastest.
Arguments:
- queries: bfloat16 [4096, 4096], P('ctx', 'ch'), may hold values from -12 to 12
- key_input: bfloat16 [4096, 4096], P('ctx', 'ch'), may hold values from -6 to 6
- value_input: bfloat16 [4096, 4096], P('ctx', 'ch'), may hold values from -6 to 6
- filters: bfloat16 [4096, 4096], P('ctx', 'ch'), may hold values from -0.3 to 0.3
- skip_gain: float32 [4096], P('ch'), may hold values from -0.3 to 0.3
- out_weight: bfloat16 [4096, 4096], P('ch'), may hold values from -0.125 to 0.125
Outputs:
- layer_out: bfloat16 [4096, 4096], P('ctx', 'ch')
All inputs are finite; a program needn't handle non-finite values.
Results may differ from a plain program's by a relative error of at most 0.019.
Values may be sent and summed in bfloat16 or wider, within the bound.
A program may use at most 320 MiB of HBM per device.

v0:
```python
import jax
import jax.numpy as jnp
from jax import lax
from jax.sharding import PartitionSpec as P

outer_radix = 64


def shifted(block, axis, distance):
    devices = range(lax.axis_size(axis))
    route = [(i - distance, i) for i in devices if i - distance in devices]
    return lax.ppermute(block, axis, route)


def split_pieces(values):
    if values.dtype == jnp.bfloat16:
        return [(values, 0)]
    high_part = values.astype(jnp.bfloat16)
    low_part = (values - high_part.astype(jnp.float32)).astype(jnp.bfloat16)
    return [(high_part, 0), (low_part, 1)]


def split_dot(form, left, right):
    total = None
    for left_piece, left_order in split_pieces(left):
        for right_piece, right_order in split_pieces(right):
            if left_order + right_order <= 1:
                term = jnp.einsum(form, left_piece, right_piece, preferred_element_type=jnp.float32)
                total = term if total is None else total + term
    return total


def angle_table(rows, columns, period):
    row_index = jnp.arange(rows, dtype=jnp.int32)[:, None]
    col_index = jnp.arange(columns, dtype=jnp.int32)[None, :]
    phases = row_index * col_index % period
    angles = phases.astype(jnp.float32) * (2.0 * jnp.pi / period)
    return (jnp.cos(angles), jnp.sin(angles))


def forward(signal, length):
    inner_len = length // outer_radix
    used_rows = signal.shape[0] // inner_len
    columns = signal.shape[1]
    folded = signal.reshape(used_rows, inner_len, columns)
    cos_outer, sin_outer = angle_table(outer_radix, used_rows, outer_radix)
    first_real = split_dot("kn,nqc->kqc", cos_outer, folded)
    first_imag = -split_dot("kn,nqc->kqc", sin_outer, folded)
    cos_twist, sin_twist = angle_table(outer_radix, inner_len, length)
    cos_twist = cos_twist[:, :, None]
    sin_twist = sin_twist[:, :, None]
    twist_real = first_real * cos_twist + first_imag * sin_twist
    twist_imag = first_imag * cos_twist - first_real * sin_twist
    cos_inner, sin_inner = angle_table(inner_len, inner_len, inner_len)
    spec_real = split_dot("kqc,qm->kmc", twist_real, cos_inner) + split_dot(
        "kqc,qm->kmc", twist_imag, sin_inner
    )
    spec_imag = split_dot("kqc,qm->kmc", twist_imag, cos_inner) - split_dot(
        "kqc,qm->kmc", twist_real, sin_inner
    )
    return (spec_real, spec_imag)


def inverse_tail(spec_real, spec_imag, length):
    inner_len = length // outer_radix
    cos_inner, sin_inner = angle_table(inner_len, inner_len, inner_len)
    back_real = split_dot("kmc,mq->kqc", spec_real, cos_inner) - split_dot(
        "kmc,mq->kqc", spec_imag, sin_inner
    )
    back_imag = split_dot("kmc,mq->kqc", spec_imag, cos_inner) + split_dot(
        "kmc,mq->kqc", spec_real, sin_inner
    )
    cos_twist, sin_twist = angle_table(outer_radix, inner_len, length)
    cos_twist = cos_twist[:, :, None]
    sin_twist = sin_twist[:, :, None]
    turn_real = back_real * cos_twist - back_imag * sin_twist
    turn_imag = back_imag * cos_twist + back_real * sin_twist
    cos_outer, sin_outer = angle_table(outer_radix, outer_radix, outer_radix)
    half_rows = outer_radix // 2
    tail_rows = split_dot("nk,kqc->nqc", cos_outer[half_rows:], turn_real) - split_dot(
        "nk,kqc->nqc", sin_outer[half_rows:], turn_imag
    )
    return tail_rows.reshape(half_rows * inner_len, -1) / length


def cycle_conv(mixed_in, filters, length):
    tok_rows, channels = mixed_in.shape
    all_segments = lax.all_gather(filters, "ctx", axis=0, tiled=True)
    padded = jnp.concatenate(
        [jnp.zeros((tok_rows, channels), all_segments.dtype), all_segments], axis=0
    )

    def add_lag(lag_index, held_block, sum_real, sum_imag):
        window = lax.dynamic_slice_in_dim(padded, lag_index * tok_rows, length, 0)
        filter_real, filter_imag = forward(window, length)
        input_real, input_imag = forward(held_block, length)
        sum_real = sum_real + input_real * filter_real - input_imag * filter_imag
        sum_imag = sum_imag + input_real * filter_imag + input_imag * filter_real
        return (sum_real, sum_imag)

    ctx_count = lax.axis_size("ctx")
    empty_spec = jnp.zeros((outer_radix, length // outer_radix, channels), jnp.float32)

    def cycle_step(lag_index, cycle_state):
        held_block, sum_real, sum_imag = cycle_state
        sum_real, sum_imag = add_lag(lag_index, held_block, sum_real, sum_imag)
        held_block = shifted(held_block, "ctx", 1)
        return (held_block, sum_real, sum_imag)

    held_block, sum_real, sum_imag = lax.fori_loop(
        0, ctx_count - 1, cycle_step, (mixed_in, empty_spec, empty_spec)
    )
    sum_real, sum_imag = add_lag(ctx_count - 1, held_block, sum_real, sum_imag)
    return inverse_tail(sum_real, sum_imag, length)


def per_device(queries, key_input, value_input, filters, skip_gain, out_weight):
    tok_rows, channels = queries.shape
    length = 2 * tok_rows
    mixed_in = (key_input.astype(jnp.float32) * value_input.astype(jnp.float32)).astype(
        jnp.bfloat16
    )
    conv = cycle_conv(mixed_in, filters, length)
    gated = (
        queries.astype(jnp.float32) * (conv + skip_gain[None, :] * mixed_in.astype(jnp.float32))
    ).astype(jnp.bfloat16)
    shares = lax.psum_scatter(
        lax.dot_general(
            out_weight, gated, (((0,), (1,)), ((), ())), preferred_element_type=jnp.float32
        ).astype(jnp.bfloat16),
        "ch",
        scatter_dimension=0,
        tiled=True,
    ).astype(jnp.float32)
    return shares.T.astype(jnp.bfloat16)


def solution(mesh):
    in_specs = (
        P("ctx", "ch"),
        P("ctx", "ch"),
        P("ctx", "ch"),
        P("ctx", "ch"),
        P("ch"),
        P("ch", None),
    )
    out_specs = P("ctx", "ch")
    return jax.shard_map(
        per_device, mesh=mesh, in_specs=in_specs, out_specs=out_specs, check_vma=False
    )
```

profile of v0, /device:TPU:0, one launch (start us, length us, event | category | flops | bytes accessed | tf_op | source)
XLA Modules:
  0.0 963.6 jit_solution(6129385879402401914)
XLA Ops:
  13.3 51.3 %all-gather.2.cloned.1.call-done = bf16[4096,512]{1,0:T(8,128)(2,1)} async-done(((bf16[1024,512]{1,0:T(8,128)(2,1)}), bf16[4096,512]{1,0:T(8,128)(2,1)}) %all-gather.2.cloned.1.call-update) | async-done | bytes 4194320 | tf_op jit(solution)/shard_map/all_gather | solution.py:88
  64.6 4.8 concatenate.3
  69.5 523.9 %while.21 = (s32[]{:T(128)}, bf16[1024,512]{1,0:T(8,128)(2,1)}, f32[64,32,512]{2,1,0:T(8,128)}, f32[64,32,512]{2,1,0:T(8,128)}, bf16[5120,512]{1,0:T(8,128)(2,1)...) while((s32[]{:T(128)}, bf16[1024,512]{1,0:T(8,128)(2,1)}, f32[64,32,512]{2,1,0:T(8,128)}, ...), condition=%wide.region_1.2_spmd.clone, body=%wide.region_0.1_spmd.clone.sunk | while | flops 2483855360 | bytes 476086720 | solution.py:110
  71.2 4.4 collective-permute-start
  80.2 4.9 fusion.855
  87.1 5.2 convolution_add_fusion.6
  98.7 11.0 %subtract_convert_fusion.35 = (bf16[64,32,512]{2,0,1:T(8,128)(2,1)}, bf16[64,32,512]{2,0,1:T(8,128)(2,1)S(1)}, bf16[64,32,512]{2,0,1:T(8,128)(2,1)S(1)}, bf16[64...) fusion(f32[64,32]{0,1:T(8,128)S(1)} %get-tuple-element.274, ...), kind=kOutput, calls=%fused_computation.9.clone.1 | convolution fusion | flops 165748736 | bytes 35667968 | tf_op jit(solution)/shard_map/while/body/eval_jaxpr/kn,nqc->kqc/dot_general | solution.py:28
  139.6 4.1 fusion.856
  169.8 3.8 fusion.868
  177.4 3.9 fusion.858
  185.1 12.3 %add_subtract_fusion.5 = f32[32,64,512]{2,0,1:T(8,128)} fusion(f32[32,64,512]{2,0,1:T(8,128)} %fusion.866, f32[32,64,512]{2,0,1:T(8,128)} %fusion.867, f32[32,64,512]{2,0,1:T(8,128)} %fusion.868, f32[32,64,512]{2,0,1:T(8,128)} %fusion.869, f32[32,64,512]{2,0,1:T(8,128)} %fusion.870, bf16[64,32,512]{2,0,1:T(8,128)(2,1)} %get-tuple-element.277), kind=kOutput, calls=%fused_computation.4.clone.1 | convolution fusion | flops 72367104 | bytes 27262976 | tf_op jit(solution)/shard_map/while/body/eval_jaxpr/kqc,qm->kmc/dot_general | solution.py:28
  197.5 10.7 %add_add_fusion.7 = f32[32,64,512]{2,0,1:T(8,128)} fusion(f32[32,64,512]{2,0,1:T(8,128)S(1)} %copy-done.8, f32[32,64,512]{2,0,1:T(8,128)} %fusion.862, f32[32,64,512]{2,0,1:T(8,128)} %fusion.863, f32[32,64,512]{2,0,1:T(8,128)} %fusion.864, f32[32,64,512]{2,0,1:T(8,128)} %fusion.865, bf16[64,32,512]{2,0,1:T(8,128)(2,1)S(1)} %copy-done.1), kind=kOutput, calls=%fused_computation.12.clone.1 | convolution fusion | flops 72367104 | bytes 27262976 | tf_op jit(solution)/shard_map/while/body/eval_jaxpr/kqc,qm->kmc/dot_general | solution.py:28
  209.7 6.9 add_add_fusion.6
  216.6 17.4 %bitcast_add_fusion.8 = (f32[64,32,512]{2,1,0:T(8,128)}, f32[64,32,512]{2,1,0:T(8,128)}) fusion(f32[64,32,512]{2,1,0:T(8,128)} %get-tuple-element.298, f32[32,64,512]{2,0,1:T(8,128)} %add_add_fusion.6, f32[32,64,512]{2,0,1:T(8,128)} %add_add_fusion.7, f32[32,64,512]{2,0,1:T(8,128)} %add_subtract_fusion.5, pred[]{:T(512)S(6)} %compare.21, ...), kind=kOutput, calls=%fused_computation.clone.1 | convolution fusion | flops 82852864 | bytes 52428800 | tf_op jit(solution)/shard_map/while/body/eval_jaxpr/kqc,qm->kmc/dot_general | solution.py:28
  243.5 4.9 fusion.855
  250.4 5.2 convolution_add_fusion.6
  262.0 21.1 %subtract_convert_fusion.35 = (bf16[64,32,512]{2,0,1:T(8,128)(2,1)}, bf16[64,32,512]{2,0,1:T(8,128)(2,1)S(1)}, bf16[64,32,512]{2,0,1:T(8,128)(2,1)S(1)}, bf16[64...) fusion(f32[64,32]{0,1:T(8,128)S(1)} %get-tuple-element.274, ...), kind=kOutput, calls=%fused_computation.9.clone.1 | convolution fusion | flops 165748736 | bytes 35667968 | tf_op jit(solution)/shard_map/while/body/eval_jaxpr/kn,nqc->kqc/dot_general | solution.py:28
  313.0 4.1 fusion.856
  343.2 3.8 fusion.868
  350.9 3.9 fusion.858
  358.5 12.3 %add_subtract_fusion.5 = f32[32,64,512]{2,0,1:T(8,128)} fusion(f32[32,64,512]{2,0,1:T(8,128)} %fusion.866, f32[32,64,512]{2,0,1:T(8,128)} %fusion.867, f32[32,64,512]{2,0,1:T(8,128)} %fusion.868, f32[32,64,512]{2,0,1:T(8,128)} %fusion.869, f32[32,64,512]{2,0,1:T(8,128)} %fusion.870, bf16[64,32,512]{2,0,1:T(8,128)(2,1)} %get-tuple-element.277), kind=kOutput, calls=%fused_computation.4.clone.1 | convolution fusion | flops 72367104 | bytes 27262976 | tf_op jit(solution)/shard_map/while/body/eval_jaxpr/kqc,qm->kmc/dot_general | solution.py:28
  370.9 10.7 %add_add_fusion.7 = f32[32,64,512]{2,0,1:T(8,128)} fusion(f32[32,64,512]{2,0,1:T(8,128)S(1)} %copy-done.8, f32[32,64,512]{2,0,1:T(8,128)} %fusion.862, f32[32,64,512]{2,0,1:T(8,128)} %fusion.863, f32[32,64,512]{2,0,1:T(8,128)} %fusion.864, f32[32,64,512]{2,0,1:T(8,128)} %fusion.865, bf16[64,32,512]{2,0,1:T(8,128)(2,1)S(1)} %copy-done.1), kind=kOutput, calls=%fused_computation.12.clone.1 | convolution fusion | flops 72367104 | bytes 27262976 | tf_op jit(solution)/shard_map/while/body/eval_jaxpr/kqc,qm->kmc/dot_general | solution.py:28
  383.1 6.9 add_add_fusion.6
  390.0 19.8 %bitcast_add_fusion.8 = (f32[64,32,512]{2,1,0:T(8,128)}, f32[64,32,512]{2,1,0:T(8,128)}) fusion(f32[64,32,512]{2,1,0:T(8,128)} %get-tuple-element.298, f32[32,64,512]{2,0,1:T(8,128)} %add_add_fusion.6, f32[32,64,512]{2,0,1:T(8,128)} %add_add_fusion.7, f32[32,64,512]{2,0,1:T(8,128)} %add_subtract_fusion.5, pred[]{:T(512)S(6)} %compare.21, ...), kind=kOutput, calls=%fused_computation.clone.1 | convolution fusion | flops 82852864 | bytes 52428800 | tf_op jit(solution)/shard_map/while/body/eval_jaxpr/kqc,qm->kmc/dot_general | solution.py:28
  418.4 4.9 fusion.855
  425.4 5.2 convolution_add_fusion.6
  437.0 21.1 %subtract_convert_fusion.35 = (bf16[64,32,512]{2,0,1:T(8,128)(2,1)}, bf16[64,32,512]{2,0,1:T(8,128)(2,1)S(1)}, bf16[64,32,512]{2,0,1:T(8,128)(2,1)S(1)}, bf16[64...) fusion(f32[64,32]{0,1:T(8,128)S(1)} %get-tuple-element.274, ...), kind=kOutput, calls=%fused_computation.9.clone.1 | convolution fusion | flops 165748736 | bytes 35667968 | tf_op jit(solution)/shard_map/while/body/eval_jaxpr/kn,nqc->kqc/dot_general | solution.py:28
  487.9 4.1 fusion.856
  525.8 3.9 fusion.858
  533.5 12.3 %add_subtract_fusion.5 = f32[32,64,512]{2,0,1:T(8,128)} fusion(f32[32,64,512]{2,0,1:T(8,128)} %fusion.866, f32[32,64,512]{2,0,1:T(8,128)} %fusion.867, f32[32,64,512]{2,0,1:T(8,128)} %fusion.868, f32[32,64,512]{2,0,1:T(8,128)} %fusion.869, f32[32,64,512]{2,0,1:T(8,128)} %fusion.870, bf16[64,32,512]{2,0,1:T(8,128)(2,1)} %get-tuple-element.277), kind=kOutput, calls=%fused_computation.4.clone.1 | convolution fusion | flops 72367104 | bytes 27262976 | tf_op jit(solution)/shard_map/while/body/eval_jaxpr/kqc,qm->kmc/dot_general | solution.py:28
  545.9 10.7 %add_add_fusion.7 = f32[32,64,512]{2,0,1:T(8,128)} fusion(f32[32,64,512]{2,0,1:T(8,128)S(1)} %copy-done.8, f32[32,64,512]{2,0,1:T(8,128)} %fusion.862, f32[32,64,512]{2,0,1:T(8,128)} %fusion.863, f32[32,64,512]{2,0,1:T(8,128)} %fusion.864, f32[32,64,512]{2,0,1:T(8,128)} %fusion.865, bf16[64,32,512]{2,0,1:T(8,128)(2,1)S(1)} %copy-done.1), kind=kOutput, calls=%fused_computation.12.clone.1 | convolution fusion | flops 72367104 | bytes 27262976 | tf_op jit(solution)/shard_map/while/body/eval_jaxpr/kqc,qm->kmc/dot_general | solution.py:28
  558.1 6.9 add_add_fusion.6
  564.9 19.8 %bitcast_add_fusion.8 = (f32[64,32,512]{2,1,0:T(8,128)}, f32[64,32,512]{2,1,0:T(8,128)}) fusion(f32[64,32,512]{2,1,0:T(8,128)} %get-tuple-element.298, f32[32,64,512]{2,0,1:T(8,128)} %add_add_fusion.6, f32[32,64,512]{2,0,1:T(8,128)} %add_add_fusion.7, f32[32,64,512]{2,0,1:T(8,128)} %add_subtract_fusion.5, pred[]{:T(512)S(6)} %compare.21, ...), kind=kOutput, calls=%fused_computation.clone.1 | convolution fusion | flops 82852864 | bytes 52428800 | tf_op jit(solution)/shard_map/while/body/eval_jaxpr/kqc,qm->kmc/dot_general | solution.py:28
  601.0 4.9 fusion.328
  605.8 4.5 convolution_add_fusion.3
  610.3 4.5 add_negate_fusion.3
  614.8 5.0 convolution_add_fusion.2
  619.8 11.0 %subtract_convert_fusion.15 = (bf16[64,32,512]{2,0,1:T(8,128)(2,1)}, bf16[64,32,512]{2,0,1:T(8,128)(2,1)S(1)}, bf16[64,32,512]{2,0,1:T(8,128)(2,1)S(1)}, bf16[64...) fusion(f32[64,32]{0,1:T(8,128)S(1)} %copy-done.23, ...), kind=kOutput, calls=%fused_computation.320 | convolution fusion | flops 165748736 | bytes 35667968 | tf_op jit(solution)/shard_map/kn,nqc->kqc/dot_general | solution.py:28
  687.0 3.9 fusion.299
  702.1 9.2 add_subtract_fusion.2
  711.3 11.7 %add_add_fusion.3 = f32[32,64,512]{2,0,1:T(8,128)} fusion(f32[32,64,512]{2,0,1:T(8,128)} %fusion.339, f32[32,64,512]{2,0,1:T(8,128)} %fusion.337, f32[32,64,512]{2,0,1:T(8,128)} %fusion.309, f32[32,64,512]{2,0,1:T(8,128)} %fusion.347, f32[32,64,512]{2,0,1:T(8,128)} %fusion.345, bf16[64,32,512]{2,0,1:T(8,128)(2,1)S(1)} %copy-done.13), kind=kOutput, calls=%fused_computation.323 | convolution fusion | flops 72367104 | bytes 27262976 | tf_op jit(solution)/shard_map/kqc,qm->kmc/dot_general | solution.py:28
  723.0 7.1 add_add_fusion.2
  730.1 19.3 %bitcast_add_fusion.3 = (f32[64,32,512]{2,1,0:T(8,128)}, f32[64,32,512]{2,1,0:T(8,128)}) fusion(f32[64,32,512]{2,1,0:T(8,128)} %get-tuple-element.167, f32[32,64,512]{2,0,1:T(8,128)} %add_add_fusion.2, f32[32,64,512]{2,0,1:T(8,128)} %add_add_fusion.3, f32[32,64,512]{2,0,1:T(8,128)} %add_subtract_fusion.2, f32[64,32,512]{2,1,0:T(8,128)} %get-tuple-element.165, ...), kind=kOutput, calls=%fused_computation.297 | convolution fusion | flops 80755712 | bytes 52428800 | tf_op jit(solution)/shard_map/kqc,qm->kmc/dot_general | solution.py:28
  749.5 6.4 fusion.417
  787.0 59.6 %fusion.356 = (bf16[64,32,512]{2,0,1:T(8,128)(2,1)S(1)}, f32[32,64,512]{2,1,0:T(8,128)}, f32[32,64,512]{2,1,0:T(8,128)}) fusion(f32[64,32]{0,1:T(8,128)S(1)} %copy-done.23, f32[64,32]{0,1:T(8,128)S(1)} %copy-done.24, f32[32,64,512]{2,0,1:T(8,128)} %fusion.417, f32[32,64,512]{2,0,1:T(8,128)} %fusion.502, f32[32,64,512]{2,0,1:T(8,128)} %fusion.419, ...), kind=kLoop, calls=%fused_computation.393 | loop fusion | flops 14680064 | bytes 60833792 | tf_op jit(solution)/shard_map/convert_element_type | solution.py:18
  846.6 3.9 fusion.354
  860.9 6.7 convert_bitcast_fusion
  867.6 88.9 %reduce-scatter.2.cloned.1.call-done = bf16[512,1024]{0,1:T(8,128)(2,1)} async-done(((bf16[4096,1024]{0,1:T(8,128)(2,1)}), bf16[512,1024]{0,1:T(8,128)(2,1)}) %reduce-scatter.2.cloned.1.call-update) | async-done | bytes 1048592 | tf_op jit(solution)/shard_map/reduce_scatter | solution.py:127
  (228 shorter events, 370.9 us)
Async XLA Ops:
  6.5 58.1 %all-gather.2.cloned.1.call-start = ((), (), s32[]{:S(2)}) async-start(), calls=%async_computation.1 | async-start | bytes 5242880 | tf_op jit(solution)/shard_map/all_gather | solution.py:88
  7.3 949.3 %reduce-scatter.2.cloned.1.call-start = ((), (), s32[]{:S(2)}) async-start(), calls=%async_computation.2 | async-start | bytes 9437184 | tf_op jit(solution)/shard_map/reduce_scatter | solution.py:127
  71.2 162.8 %collective-permute-start = (bf16[1024,512]{1,0:T(8,128)(2,1)S(1)}, bf16[1024,512]{1,0:T(8,128)(2,1)}, u32[]{:S(2)}, u32[]{:S(2)}) collective-permute-start(bf16[1024,512]{1,0:T(8,128)(2,1)S(1)} %copy.397), channel_id=1, source_target_pairs={{0,8},{8,16},{16,24},{1,9},{9,17},{17,25},{2,10},{10,18},{18,26},{... | collective-permute-start | bytes 3145736 | tf_op jit(solution)/shard_map/while/body/eval_jaxpr/ppermute | solution.py:12
  169.8 3.8 copy-start.3
  173.6 3.8 copy-start.2
  177.4 3.9 copy-start
  185.1 12.4 %copy-start.1 = (bf16[64,32,512]{2,0,1:T(8,128)(2,1)S(1)}, bf16[64,32,512]{2,0,1:T(8,128)(2,1)}, u32[]{:S(2)}) copy-start(bf16[64,32,512]{2,0,1:T(8,128)(2,1)} %get-tuple-element.283) | copy-start | bytes 6291460 | tf_op jit(solution)/shard_map/while
  185.1 12.4 %copy-start.8 = (f32[32,64,512]{2,0,1:T(8,128)S(1)}, f32[32,64,512]{2,0,1:T(8,128)}, u32[]{:S(2)}) copy-start(f32[32,64,512]{2,0,1:T(8,128)} %fusion.861) | copy-start | bytes 12582916 | tf_op jit(solution)/shard_map/while
  197.5 10.7 %copy-start.4 = (f32[32,64,512]{2,0,1:T(8,128)S(1)}, f32[32,64,512]{2,0,1:T(8,128)}, u32[]{:S(2)}) copy-start(f32[32,64,512]{2,0,1:T(8,128)} %fusion.856) | copy-start | bytes 12582916 | tf_op jit(solution)/shard_map/while
  197.5 10.7 %copy-start.5 = (f32[32,64,512]{2,0,1:T(8,128)S(1)}, f32[32,64,512]{2,0,1:T(8,128)}, u32[]{:S(2)}) copy-start(f32[32,64,512]{2,0,1:T(8,128)} %fusion.857) | copy-start | bytes 12582916 | tf_op jit(solution)/shard_map/while
  197.5 10.7 %copy-start.6 = (f32[32,64,512]{2,0,1:T(8,128)S(1)}, f32[32,64,512]{2,0,1:T(8,128)}, u32[]{:S(2)}) copy-start(f32[32,64,512]{2,0,1:T(8,128)} %fusion.859) | copy-start | bytes 12582916 | tf_op jit(solution)/shard_map/while
  197.5 12.2 %copy-start.7 = (f32[32,64,512]{2,0,1:T(8,128)S(1)}, f32[32,64,512]{2,0,1:T(8,128)}, u32[]{:S(2)}) copy-start(f32[32,64,512]{2,0,1:T(8,128)} %fusion.860) | copy-start | bytes 12582916 | tf_op jit(solution)/shard_map/while
  235.5 174.3 %collective-permute-start = (bf16[1024,512]{1,0:T(8,128)(2,1)S(1)}, bf16[1024,512]{1,0:T(8,128)(2,1)}, u32[]{:S(2)}, u32[]{:S(2)}) collective-permute-start(bf16[1024,512]{1,0:T(8,128)(2,1)S(1)} %copy.397), channel_id=1, source_target_pairs={{0,8},{8,16},{16,24},{1,9},{9,17},{17,25},{2,10},{10,18},{18,26},{... | collective-permute-start | bytes 3145736 | tf_op jit(solution)/shard_map/while/body/eval_jaxpr/ppermute | solution.py:12
  343.2 3.8 copy-start.3
  347.1 3.8 copy-start.2
  350.9 3.9 copy-start
  358.5 12.4 %copy-start.1 = (bf16[64,32,512]{2,0,1:T(8,128)(2,1)S(1)}, bf16[64,32,512]{2,0,1:T(8,128)(2,1)}, u32[]{:S(2)}) copy-start(bf16[64,32,512]{2,0,1:T(8,128)(2,1)} %get-tuple-element.283) | copy-start | bytes 6291460 | tf_op jit(solution)/shard_map/while
  358.5 12.4 %copy-start.8 = (f32[32,64,512]{2,0,1:T(8,128)S(1)}, f32[32,64,512]{2,0,1:T(8,128)}, u32[]{:S(2)}) copy-start(f32[32,64,512]{2,0,1:T(8,128)} %fusion.861) | copy-start | bytes 12582916 | tf_op jit(solution)/shard_map/while
  370.9 10.7 %copy-start.4 = (f32[32,64,512]{2,0,1:T(8,128)S(1)}, f32[32,64,512]{2,0,1:T(8,128)}, u32[]{:S(2)}) copy-start(f32[32,64,512]{2,0,1:T(8,128)} %fusion.856) | copy-start | bytes 12582916 | tf_op jit(solution)/shard_map/while
  370.9 10.7 %copy-start.5 = (f32[32,64,512]{2,0,1:T(8,128)S(1)}, f32[32,64,512]{2,0,1:T(8,128)}, u32[]{:S(2)}) copy-start(f32[32,64,512]{2,0,1:T(8,128)} %fusion.857) | copy-start | bytes 12582916 | tf_op jit(solution)/shard_map/while
  370.9 10.7 %copy-start.6 = (f32[32,64,512]{2,0,1:T(8,128)S(1)}, f32[32,64,512]{2,0,1:T(8,128)}, u32[]{:S(2)}) copy-start(f32[32,64,512]{2,0,1:T(8,128)} %fusion.859) | copy-start | bytes 12582916 | tf_op jit(solution)/shard_map/while
  370.9 12.2 %copy-start.7 = (f32[32,64,512]{2,0,1:T(8,128)S(1)}, f32[32,64,512]{2,0,1:T(8,128)}, u32[]{:S(2)}) copy-start(f32[32,64,512]{2,0,1:T(8,128)} %fusion.860) | copy-start | bytes 12582916 | tf_op jit(solution)/shard_map/while
  411.4 173.4 %collective-permute-start = (bf16[1024,512]{1,0:T(8,128)(2,1)S(1)}, bf16[1024,512]{1,0:T(8,128)(2,1)}, u32[]{:S(2)}, u32[]{:S(2)}) collective-permute-start(bf16[1024,512]{1,0:T(8,128)(2,1)S(1)} %copy.397), channel_id=1, source_target_pairs={{0,8},{8,16},{16,24},{1,9},{9,17},{17,25},{2,10},{10,18},{18,26},{... | collective-permute-start | bytes 3145736 | tf_op jit(solution)/shard_map/while/body/eval_jaxpr/ppermute | solution.py:12
  518.2 3.8 copy-start.3
  522.0 3.8 copy-start.2
  525.8 3.9 copy-start
  533.5 12.4 %copy-start.1 = (bf16[64,32,512]{2,0,1:T(8,128)(2,1)S(1)}, bf16[64,32,512]{2,0,1:T(8,128)(2,1)}, u32[]{:S(2)}) copy-start(bf16[64,32,512]{2,0,1:T(8,128)(2,1)} %get-tuple-element.283) | copy-start | bytes 6291460 | tf_op jit(solution)/shard_map/while
  533.5 12.4 %copy-start.8 = (f32[32,64,512]{2,0,1:T(8,128)S(1)}, f32[32,64,512]{2,0,1:T(8,128)}, u32[]{:S(2)}) copy-start(f32[32,64,512]{2,0,1:T(8,128)} %fusion.861) | copy-start | bytes 12582916 | tf_op jit(solution)/shard_map/while
  545.8 10.7 %copy-start.4 = (f32[32,64,512]{2,0,1:T(8,128)S(1)}, f32[32,64,512]{2,0,1:T(8,128)}, u32[]{:S(2)}) copy-start(f32[32,64,512]{2,0,1:T(8,128)} %fusion.856) | copy-start | bytes 12582916 | tf_op jit(solution)/shard_map/while
  545.8 10.7 %copy-start.5 = (f32[32,64,512]{2,0,1:T(8,128)S(1)}, f32[32,64,512]{2,0,1:T(8,128)}, u32[]{:S(2)}) copy-start(f32[32,64,512]{2,0,1:T(8,128)} %fusion.857) | copy-start | bytes 12582916 | tf_op jit(solution)/shard_map/while
  545.9 10.7 %copy-start.6 = (f32[32,64,512]{2,0,1:T(8,128)S(1)}, f32[32,64,512]{2,0,1:T(8,128)}, u32[]{:S(2)}) copy-start(f32[32,64,512]{2,0,1:T(8,128)} %fusion.859) | copy-start | bytes 12582916 | tf_op jit(solution)/shard_map/while
  545.9 12.2 %copy-start.7 = (f32[32,64,512]{2,0,1:T(8,128)S(1)}, f32[32,64,512]{2,0,1:T(8,128)}, u32[]{:S(2)}) copy-start(f32[32,64,512]{2,0,1:T(8,128)} %fusion.860) | copy-start | bytes 12582916 | tf_op jit(solution)/shard_map/while
  593.4 4.6 copy-start.21
  614.8 5.0 copy-start.23
  614.8 5.0 copy-start.24
  690.9 3.7 copy-start.14
  694.6 3.7 copy-start.13
  694.6 7.5 copy-start.18
  698.4 3.7 copy-start.17
  711.3 11.7 %copy-start.15 = (f32[32,64,512]{2,0,1:T(8,128)S(1)}, f32[32,64,512]{2,0,1:T(8,128)}, u32[]{:S(2)}) copy-start(f32[32,64,512]{2,0,1:T(8,128)} %fusion.317) | copy-start | bytes 12582916
  711.3 11.7 %copy-start.16 = (f32[32,64,512]{2,0,1:T(8,128)S(1)}, f32[32,64,512]{2,0,1:T(8,128)}, u32[]{:S(2)}) copy-start(f32[32,64,512]{2,0,1:T(8,128)} %fusion.325) | copy-start | bytes 12582916
  749.4 6.4 copy-start.10
  755.9 3.4 copy-start.9
  846.6 3.9 copy-start.25
  850.5 2.2 copy-start.11
  850.5 3.5 copy-start.12
  850.5 3.5 copy-start.26
  858.1 2.8 copy-start.28
  (4 other events, 5.3 us)
Sparse Core Ops, SparseCore 0:
  9.2 55.3 all-gather.1
  867.8 88.6 reduce-scatter.1
where the time goes:
time: 966 us; the launch traced here: 964 us
  matrix products  694 us (72%)
  waiting for transfers between devices  141 us (15%)
  other arithmetic  68.2 us (7%)
  local copies, waits for them, and re-layouts  26 us (3%)
  between operations  13.9 us (1%)
  starting transfers between devices  10.3 us (1%)
  loops' own time  10 us (1%)
    dot_general x146, matrix products, split_dot(): jnp.einsum(form, left_piece, right_piece, preferred_element_type=jnp.floa...  688 us
    reduce_scatter x1, waiting for transfers between devices, per_device(): lax.psum_scatter(lax.dot_general(out_weight, gated, (((0,), (1,)), ((), (...  88.9 us
    convert_element_type x2, other arithmetic, split_pieces(): high_part = values.astype(jnp.bfloat16)  63.5 us
    all_gather x1, waiting for transfers between devices, cycle_conv(): all_segments = lax.all_gather(filters, 'ctx', axis=0, tiled=True)  51.3 us
  transfers between devices with their start and end apart: 5, of which 2 were waited for; matrix products, arithmetic and copies ran while one was open for 52% of the time, Pallas kernels for 0%

commit v1 on v0

--- a/solution.py
+++ b/solution.py
@@ -85,7 +85,12 @@
 
 def cycle_conv(mixed_in, filters, length):
     tok_rows, channels = mixed_in.shape
-    all_segments = lax.all_gather(filters, "ctx", axis=0, tiled=True)
+    ring = [filters]
+    for hop in range(3):
+        ring.append(lax.ppermute(ring[-1], "ctx", [(dev, (dev + 1) % 4) for dev in range(4)]))
+    all_segments = jnp.roll(
+        jnp.concatenate(ring[::-1], axis=0), (lax.axis_index("ctx") + 1) * ring[0].shape[0], axis=0
+    )
     padded = jnp.concatenate(
         [jnp.zeros((tok_rows, channels), all_segments.dtype), all_segments], axis=0
     )

time: 966 us -> 981 us (1.016)
  waiting for transfers between devices: 141 us -> 156 us
    ppermute x0 -> x3, waiting for transfers between devices: none -> 67.2 us  [cycle_conv(): lax.ppermute(ring[-1], 'ctx', [(dev, (dev + 1) % 4) for dev in range(4)])]
    all_gather x1 -> x0, waiting for transfers between devices: 51.3 us -> none  [cycle_conv(): all_segments = lax.all_gather(filters, 'ctx', axis=0, tiled=True)]
  transfers between devices with their start and end apart: 5 -> 7, of which waited for: 2 -> 4; matrix products, arithmetic and copies ran while one was open for 52% -> 49% of each run, Pallas kernels for 0% -> 0%
where the time goes in v1:
time: 981 us; the launch traced here: 978 us
  matrix products  685 us (70%)
  waiting for transfers between devices  156 us (16%)
  other arithmetic  68.2 us (7%)
  local copies, waits for them, and re-layouts  31.7 us (3%)
  between operations  13.9 us (1%)
  starting transfers between devices  13.4 us (1%)
    dot_general x146, matrix products, split_dot(): jnp.einsum(form, left_piece, right_piece, preferred_element_type=jnp.floa...  678 us
    reduce_scatter x1, waiting for transfers between devices, per_device(): lax.psum_scatter(lax.dot_general(out_weight, gated, (((0,), (1,)), ((), (...  89.1 us
    ppermute x3, waiting for transfers between devices, cycle_conv(): lax.ppermute(ring[-1], 'ctx', [(dev, (dev + 1) % 4) for dev in range(4)])  67.2 us
    convert_element_type x2, other arithmetic, split_pieces(): high_part = values.astype(jnp.bfloat16)  63.5 us
  transfers between devices with their start and end apart: 7, of which 4 were waited for; matrix products, arithmetic and copies ran while one was open for 49% of the time, Pallas kernels for 0%

profile of v1, /device:TPU:0, one launch (start us, length us, event | category | flops | bytes accessed | tf_op | source)
XLA Modules:
  0.0 977.9 jit_solution(11011523382794742809)
XLA Ops:
  9.5 24.3 %collective-permute-done.1 = bf16[1024,512]{1,0:T(8,128)(2,1)S(1)} collective-permute-done((bf16[1024,512]{1,0:T(8,128)(2,1)}, bf16[1024,512]{1,0:T(8,128)(2,1)S(1)}, u32[]{:S(2)}, u32[]{:S(2)}) %collective-permute-start.1) | collective-permute-done | bytes 1048608 | tf_op jit(solution)/shard_map/ppermute | solution.py:90
  34.6 24.5 %collective-permute-done.2 = bf16[1024,512]{1,0:T(8,128)(2,1)S(1)} collective-permute-done((bf16[1024,512]{1,0:T(8,128)(2,1)S(1)}, bf16[1024,512]{1,0:T(8,128)(2,1)S(1)}, u32[]{:S(2)}, u32[]{:S(2)}) %collective-permute-start.2) | collective-permute-done | bytes 1048608 | tf_op jit(solution)/shard_map/ppermute | solution.py:90
  65.1 18.4 %collective-permute-done.3 = bf16[1024,512]{1,0:T(8,128)(2,1)} collective-permute-done((bf16[1024,512]{1,0:T(8,128)(2,1)S(1)}, bf16[1024,512]{1,0:T(8,128)(2,1)}, u32[]{:S(2)}, u32[]{:S(2)}) %collective-permute-start.3) | collective-permute-done | bytes 1048608 | tf_op jit(solution)/shard_map/ppermute | solution.py:90
  92.5 503.1 %while.21 = (s32[]{:T(128)}, bf16[1024,512]{1,0:T(8,128)(2,1)}, f32[64,32,512]{2,1,0:T(8,128)}, f32[64,32,512]{2,1,0:T(8,128)}, bf16[5120,512]{1,0:T(8,128)(2,1)...) while((s32[]{:T(128)}, bf16[1024,512]{1,0:T(8,128)(2,1)}, f32[64,32,512]{2,1,0:T(8,128)}, ...), condition=%wide.region_1.2_spmd.clone, body=%wide.region_0.1_spmd.clone.sunk | while | flops 2483855360 | bytes 476086720 | solution.py:115
  100.8 4.9 fusion.855
  107.8 5.0 convolution_add_fusion.6
  119.3 11.3 %subtract_convert_fusion.35 = (bf16[64,32,512]{2,0,1:T(8,128)(2,1)}, bf16[64,32,512]{2,0,1:T(8,128)(2,1)S(1)}, bf16[64,32,512]{2,0,1:T(8,128)(2,1)S(1)}, bf16[64...) fusion(f32[64,32]{0,1:T(8,128)S(1)} %get-tuple-element.274, ...), kind=kOutput, calls=%fused_computation.9.clone.1 | convolution fusion | flops 165748736 | bytes 35667968 | tf_op jit(solution)/shard_map/while/body/eval_jaxpr/kn,nqc->kqc/dot_general | solution.py:28
  141.9 3.9 fusion.870
  190.7 3.9 fusion.868
  205.8 12.4 %add_subtract_fusion.5 = f32[32,64,512]{2,0,1:T(8,128)} fusion(f32[32,64,512]{2,0,1:T(8,128)} %fusion.866, f32[32,64,512]{2,0,1:T(8,128)} %fusion.867, f32[32,64,512]{2,0,1:T(8,128)} %fusion.868, f32[32,64,512]{2,0,1:T(8,128)} %fusion.869, f32[32,64,512]{2,0,1:T(8,128)} %fusion.870, bf16[64,32,512]{2,0,1:T(8,128)(2,1)} %get-tuple-element.277), kind=kOutput, calls=%fused_computation.4.clone.1 | convolution fusion | flops 72367104 | bytes 27262976 | tf_op jit(solution)/shard_map/while/body/eval_jaxpr/kqc,qm->kmc/dot_general | solution.py:28
  218.2 10.7 %add_add_fusion.7 = f32[32,64,512]{2,0,1:T(8,128)} fusion(f32[32,64,512]{2,0,1:T(8,128)S(1)} %copy-done.8, f32[32,64,512]{2,0,1:T(8,128)} %fusion.862, f32[32,64,512]{2,0,1:T(8,128)} %fusion.863, f32[32,64,512]{2,0,1:T(8,128)} %fusion.864, f32[32,64,512]{2,0,1:T(8,128)} %fusion.865, bf16[64,32,512]{2,0,1:T(8,128)(2,1)S(1)} %copy-done.1), kind=kOutput, calls=%fused_computation.12.clone.1 | convolution fusion | flops 72367104 | bytes 27262976 | tf_op jit(solution)/shard_map/while/body/eval_jaxpr/kqc,qm->kmc/dot_general | solution.py:28
  230.4 6.7 add_add_fusion.6
  237.1 17.7 %bitcast_add_fusion.8 = (f32[64,32,512]{2,1,0:T(8,128)}, f32[64,32,512]{2,1,0:T(8,128)}) fusion(f32[64,32,512]{2,1,0:T(8,128)} %get-tuple-element.298, f32[32,64,512]{2,0,1:T(8,128)} %add_add_fusion.6, f32[32,64,512]{2,0,1:T(8,128)} %add_add_fusion.7, f32[32,64,512]{2,0,1:T(8,128)} %add_subtract_fusion.5, pred[]{:T(512)S(6)} %compare.22, ...), kind=kOutput, calls=%fused_computation.clone.1 | convolution fusion | flops 82852864 | bytes 52428800 | tf_op jit(solution)/shard_map/while/body/eval_jaxpr/kqc,qm->kmc/dot_general | solution.py:28
  256.3 5.1 collective-permute-start
  266.0 4.9 fusion.855
  272.9 5.0 convolution_add_fusion.6
  284.5 11.3 %subtract_convert_fusion.35 = (bf16[64,32,512]{2,0,1:T(8,128)(2,1)}, bf16[64,32,512]{2,0,1:T(8,128)(2,1)S(1)}, bf16[64,32,512]{2,0,1:T(8,128)(2,1)S(1)}, bf16[64...) fusion(f32[64,32]{0,1:T(8,128)S(1)} %get-tuple-element.274, ...), kind=kOutput, calls=%fused_computation.9.clone.1 | convolution fusion | flops 165748736 | bytes 35667968 | tf_op jit(solution)/shard_map/while/body/eval_jaxpr/kn,nqc->kqc/dot_general | solution.py:28
  307.1 3.9 fusion.870
  325.9 3.9 fusion.856
  355.9 3.9 fusion.868
  370.9 12.4 %add_subtract_fusion.5 = f32[32,64,512]{2,0,1:T(8,128)} fusion(f32[32,64,512]{2,0,1:T(8,128)} %fusion.866, f32[32,64,512]{2,0,1:T(8,128)} %fusion.867, f32[32,64,512]{2,0,1:T(8,128)} %fusion.868, f32[32,64,512]{2,0,1:T(8,128)} %fusion.869, f32[32,64,512]{2,0,1:T(8,128)} %fusion.870, bf16[64,32,512]{2,0,1:T(8,128)(2,1)} %get-tuple-element.277), kind=kOutput, calls=%fused_computation.4.clone.1 | convolution fusion | flops 72367104 | bytes 27262976 | tf_op jit(solution)/shard_map/while/body/eval_jaxpr/kqc,qm->kmc/dot_general | solution.py:28
  383.4 10.7 %add_add_fusion.7 = f32[32,64,512]{2,0,1:T(8,128)} fusion(f32[32,64,512]{2,0,1:T(8,128)S(1)} %copy-done.8, f32[32,64,512]{2,0,1:T(8,128)} %fusion.862, f32[32,64,512]{2,0,1:T(8,128)} %fusion.863, f32[32,64,512]{2,0,1:T(8,128)} %fusion.864, f32[32,64,512]{2,0,1:T(8,128)} %fusion.865, bf16[64,32,512]{2,0,1:T(8,128)(2,1)S(1)} %copy-done.1), kind=kOutput, calls=%fused_computation.12.clone.1 | convolution fusion | flops 72367104 | bytes 27262976 | tf_op jit(solution)/shard_map/while/body/eval_jaxpr/kqc,qm->kmc/dot_general | solution.py:28
  395.5 6.7 add_add_fusion.6
  402.3 20.1 %bitcast_add_fusion.8 = (f32[64,32,512]{2,1,0:T(8,128)}, f32[64,32,512]{2,1,0:T(8,128)}) fusion(f32[64,32,512]{2,1,0:T(8,128)} %get-tuple-element.298, f32[32,64,512]{2,0,1:T(8,128)} %add_add_fusion.6, f32[32,64,512]{2,0,1:T(8,128)} %add_add_fusion.7, f32[32,64,512]{2,0,1:T(8,128)} %add_subtract_fusion.5, pred[]{:T(512)S(6)} %compare.22, ...), kind=kOutput, calls=%fused_computation.clone.1 | convolution fusion | flops 82852864 | bytes 52428800 | tf_op jit(solution)/shard_map/while/body/eval_jaxpr/kqc,qm->kmc/dot_general | solution.py:28
  430.7 4.9 fusion.855
  437.7 5.0 convolution_add_fusion.6
  449.2 11.3 %subtract_convert_fusion.35 = (bf16[64,32,512]{2,0,1:T(8,128)(2,1)}, bf16[64,32,512]{2,0,1:T(8,128)(2,1)S(1)}, bf16[64,32,512]{2,0,1:T(8,128)(2,1)S(1)}, bf16[64...) fusion(f32[64,32]{0,1:T(8,128)S(1)} %get-tuple-element.274, ...), kind=kOutput, calls=%fused_computation.9.clone.1 | convolution fusion | flops 165748736 | bytes 35667968 | tf_op jit(solution)/shard_map/while/body/eval_jaxpr/kn,nqc->kqc/dot_general | solution.py:28
  471.8 3.9 fusion.870
  520.6 3.9 fusion.868
  535.7 12.4 %add_subtract_fusion.5 = f32[32,64,512]{2,0,1:T(8,128)} fusion(f32[32,64,512]{2,0,1:T(8,128)} %fusion.866, f32[32,64,512]{2,0,1:T(8,128)} %fusion.867, f32[32,64,512]{2,0,1:T(8,128)} %fusion.868, f32[32,64,512]{2,0,1:T(8,128)} %fusion.869, f32[32,64,512]{2,0,1:T(8,128)} %fusion.870, bf16[64,32,512]{2,0,1:T(8,128)(2,1)} %get-tuple-element.277), kind=kOutput, calls=%fused_computation.4.clone.1 | convolution fusion | flops 72367104 | bytes 27262976 | tf_op jit(solution)/shard_map/while/body/eval_jaxpr/kqc,qm->kmc/dot_general | solution.py:28
  548.1 10.7 %add_add_fusion.7 = f32[32,64,512]{2,0,1:T(8,128)} fusion(f32[32,64,512]{2,0,1:T(8,128)S(1)} %copy-done.8, f32[32,64,512]{2,0,1:T(8,128)} %fusion.862, f32[32,64,512]{2,0,1:T(8,128)} %fusion.863, f32[32,64,512]{2,0,1:T(8,128)} %fusion.864, f32[32,64,512]{2,0,1:T(8,128)} %fusion.865, bf16[64,32,512]{2,0,1:T(8,128)(2,1)S(1)} %copy-done.1), kind=kOutput, calls=%fused_computation.12.clone.1 | convolution fusion | flops 72367104 | bytes 27262976 | tf_op jit(solution)/shard_map/while/body/eval_jaxpr/kqc,qm->kmc/dot_general | solution.py:28
  560.3 6.7 add_add_fusion.6
  567.0 20.1 %bitcast_add_fusion.8 = (f32[64,32,512]{2,1,0:T(8,128)}, f32[64,32,512]{2,1,0:T(8,128)}) fusion(f32[64,32,512]{2,1,0:T(8,128)} %get-tuple-element.298, f32[32,64,512]{2,0,1:T(8,128)} %add_add_fusion.6, f32[32,64,512]{2,0,1:T(8,128)} %add_add_fusion.7, f32[32,64,512]{2,0,1:T(8,128)} %add_subtract_fusion.5, pred[]{:T(512)S(6)} %compare.22, ...), kind=kOutput, calls=%fused_computation.clone.1 | convolution fusion | flops 82852864 | bytes 52428800 | tf_op jit(solution)/shard_map/while/body/eval_jaxpr/kqc,qm->kmc/dot_general | solution.py:28
  604.7 4.9 fusion.328
  609.6 4.5 convolution_add_fusion.3
  614.0 4.5 add_negate_fusion.3
  618.5 5.0 convolution_add_fusion.2
  623.5 21.2 %subtract_convert_fusion.15 = (bf16[64,32,512]{2,0,1:T(8,128)(2,1)}, bf16[64,32,512]{2,0,1:T(8,128)(2,1)S(1)}, bf16[64,32,512]{2,0,1:T(8,128)(2,1)S(1)}, bf16[64...) fusion(f32[64,32]{0,1:T(8,128)S(1)} %copy-done.24, ...), kind=kOutput, calls=%fused_computation.320 | convolution fusion | flops 165748736 | bytes 35667968 | tf_op jit(solution)/shard_map/kn,nqc->kqc/dot_general | solution.py:28
  701.1 3.9 fusion.299
  716.2 9.2 add_subtract_fusion.2
  725.4 11.7 %add_add_fusion.3 = f32[32,64,512]{2,0,1:T(8,128)} fusion(f32[32,64,512]{2,0,1:T(8,128)} %fusion.339, f32[32,64,512]{2,0,1:T(8,128)} %fusion.337, f32[32,64,512]{2,0,1:T(8,128)} %fusion.309, f32[32,64,512]{2,0,1:T(8,128)} %fusion.347, f32[32,64,512]{2,0,1:T(8,128)} %fusion.345, bf16[64,32,512]{2,0,1:T(8,128)(2,1)S(1)} %copy-done.13), kind=kOutput, calls=%fused_computation.323 | convolution fusion | flops 72367104 | bytes 27262976 | tf_op jit(solution)/shard_map/kqc,qm->kmc/dot_general | solution.py:28
  737.1 7.1 add_add_fusion.2
  744.2 19.3 %bitcast_add_fusion.3 = (f32[64,32,512]{2,1,0:T(8,128)}, f32[64,32,512]{2,1,0:T(8,128)}) fusion(f32[64,32,512]{2,1,0:T(8,128)} %get-tuple-element.167, f32[32,64,512]{2,0,1:T(8,128)} %add_add_fusion.2, f32[32,64,512]{2,0,1:T(8,128)} %add_add_fusion.3, f32[32,64,512]{2,0,1:T(8,128)} %add_subtract_fusion.2, f32[64,32,512]{2,1,0:T(8,128)} %get-tuple-element.165, ...), kind=kOutput, calls=%fused_computation.297 | convolution fusion | flops 80755712 | bytes 52428800 | tf_op jit(solution)/shard_map/kqc,qm->kmc/dot_general | solution.py:28
  763.5 6.4 fusion.417
  801.0 59.6 %fusion.356 = (bf16[64,32,512]{2,0,1:T(8,128)(2,1)S(1)}, f32[32,64,512]{2,1,0:T(8,128)}, f32[32,64,512]{2,1,0:T(8,128)}) fusion(f32[64,32]{0,1:T(8,128)S(1)} %copy-done.24, f32[64,32]{0,1:T(8,128)S(1)} %copy-done.25, f32[32,64,512]{2,0,1:T(8,128)} %fusion.417, f32[32,64,512]{2,0,1:T(8,128)} %fusion.502, f32[32,64,512]{2,0,1:T(8,128)} %fusion.419, ...), kind=kLoop, calls=%fused_computation.393 | loop fusion | flops 14680064 | bytes 60833792 | tf_op jit(solution)/shard_map/convert_element_type | solution.py:18
  860.6 3.9 fusion.354
  874.8 6.9 convert_bitcast_fusion
  881.7 89.1 %reduce-scatter.2.cloned.1.call-done = bf16[512,1024]{0,1:T(8,128)(2,1)} async-done(((bf16[4096,1024]{0,1:T(8,128)(2,1)}), bf16[512,1024]{0,1:T(8,128)(2,1)}) %reduce-scatter.2.cloned.1.call-update) | async-done | bytes 1048592 | tf_op jit(solution)/shard_map/reduce_scatter | solution.py:132
  (242 shorter events, 387.1 us)
Async XLA Ops:
  6.5 964.3 %reduce-scatter.2.cloned.1.call-start = ((), (), s32[]{:S(2)}) async-start(), calls=%async_computation.1 | async-start | bytes 9437184 | tf_op jit(solution)/shard_map/reduce_scatter | solution.py:132
  6.5 27.3 %collective-permute-start.1 = (bf16[1024,512]{1,0:T(8,128)(2,1)}, bf16[1024,512]{1,0:T(8,128)(2,1)S(1)}, u32[]{:S(2)}, u32[]{:S(2)}) collective-permute-start(bf16[1024,512]{1,0:T(8,128)(2,1)} %param.11), channel_id=1, source_target_pairs={{0,8},{8,16},{16,24},{24,0},{1,9},{9,17},{17,25},{25,1},{2,10},{10... | collective-permute-start | bytes 3145736 | tf_op jit(solution)/shard_map/ppermute | solution.py:90
  33.8 25.2 %collective-permute-start.2 = (bf16[1024,512]{1,0:T(8,128)(2,1)S(1)}, bf16[1024,512]{1,0:T(8,128)(2,1)S(1)}, u32[]{:S(2)}, u32[]{:S(2)}) collective-permute-start(bf16[1024,512]{1,0:T(8,128)(2,1)S(1)} %collective-permute-done.1), channel_id=1, source_target_pairs={{0,8},{8,16},{16,24},{24,0},{1,9},{9,17},{17,25},{25,1},{2,10},{10... | collective-permute-start | bytes 3145736 | tf_op jit(solution)/shard_map/ppermute | solution.py:90
  59.0 24.4 %collective-permute-start.3 = (bf16[1024,512]{1,0:T(8,128)(2,1)S(1)}, bf16[1024,512]{1,0:T(8,128)(2,1)}, u32[]{:S(2)}, u32[]{:S(2)}) collective-permute-start(bf16[1024,512]{1,0:T(8,128)(2,1)S(1)} %collective-permute-done.2), channel_id=1, source_target_pairs={{0,8},{8,16},{16,24},{24,0},{1,9},{9,17},{17,25},{25,1},{2,10},{10... | collective-permute-start | bytes 3145736 | tf_op jit(solution)/shard_map/ppermute | solution.py:90
  61.9 23.1 %copy-start.22 = (bf16[1024,512]{1,0:T(8,128)(2,1)S(1)}, bf16[1024,512]{1,0:T(8,128)(2,1)}, u32[]{:S(2)}) copy-start(bf16[1024,512]{1,0:T(8,128)(2,1)} %param.11) | copy-start | bytes 3145732
  93.9 160.9 %collective-permute-start = (bf16[1024,512]{1,0:T(8,128)(2,1)S(1)}, bf16[1024,512]{1,0:T(8,128)(2,1)}, u32[]{:S(2)}, u32[]{:S(2)}) collective-permute-start(bf16[1024,512]{1,0:T(8,128)(2,1)S(1)} %copy.404), channel_id=1, source_target_pairs={{0,8},{8,16},{16,24},{1,9},{9,17},{17,25},{2,10},{10,18},{18,26},{... | collective-permute-start | bytes 3145736 | tf_op jit(solution)/shard_map/while/body/eval_jaxpr/ppermute | solution.py:12
  190.7 3.9 copy-start.3
  194.6 3.7 copy-start.2
  198.3 3.7 copy-start
  205.8 12.4 %copy-start.1 = (bf16[64,32,512]{2,0,1:T(8,128)(2,1)S(1)}, bf16[64,32,512]{2,0,1:T(8,128)(2,1)}, u32[]{:S(2)}) copy-start(bf16[64,32,512]{2,0,1:T(8,128)(2,1)} %get-tuple-element.283) | copy-start | bytes 6291460 | tf_op jit(solution)/shard_map/while
  205.8 12.4 %copy-start.8 = (f32[32,64,512]{2,0,1:T(8,128)S(1)}, f32[32,64,512]{2,0,1:T(8,128)}, u32[]{:S(2)}) copy-start(f32[32,64,512]{2,0,1:T(8,128)} %fusion.861) | copy-start | bytes 12582916 | tf_op jit(solution)/shard_map/while
  218.2 10.7 %copy-start.4 = (f32[32,64,512]{2,0,1:T(8,128)S(1)}, f32[32,64,512]{2,0,1:T(8,128)}, u32[]{:S(2)}) copy-start(f32[32,64,512]{2,0,1:T(8,128)} %fusion.856) | copy-start | bytes 12582916 | tf_op jit(solution)/shard_map/while
  218.2 10.7 %copy-start.5 = (f32[32,64,512]{2,0,1:T(8,128)S(1)}, f32[32,64,512]{2,0,1:T(8,128)}, u32[]{:S(2)}) copy-start(f32[32,64,512]{2,0,1:T(8,128)} %fusion.857) | copy-start | bytes 12582916 | tf_op jit(solution)/shard_map/while
  218.2 10.7 %copy-start.6 = (f32[32,64,512]{2,0,1:T(8,128)S(1)}, f32[32,64,512]{2,0,1:T(8,128)}, u32[]{:S(2)}) copy-start(f32[32,64,512]{2,0,1:T(8,128)} %fusion.859) | copy-start | bytes 12582916 | tf_op jit(solution)/shard_map/while
  218.2 12.2 %copy-start.7 = (f32[32,64,512]{2,0,1:T(8,128)S(1)}, f32[32,64,512]{2,0,1:T(8,128)}, u32[]{:S(2)}) copy-start(f32[32,64,512]{2,0,1:T(8,128)} %fusion.860) | copy-start | bytes 12582916 | tf_op jit(solution)/shard_map/while
  256.3 166.1 %collective-permute-start = (bf16[1024,512]{1,0:T(8,128)(2,1)S(1)}, bf16[1024,512]{1,0:T(8,128)(2,1)}, u32[]{:S(2)}, u32[]{:S(2)}) collective-permute-start(bf16[1024,512]{1,0:T(8,128)(2,1)S(1)} %copy.404), channel_id=1, source_target_pairs={{0,8},{8,16},{16,24},{1,9},{9,17},{17,25},{2,10},{10,18},{18,26},{... | collective-permute-start | bytes 3145736 | tf_op jit(solution)/shard_map/while/body/eval_jaxpr/ppermute | solution.py:12
  355.9 3.9 copy-start.3
  359.8 3.7 copy-start.2
  363.5 3.7 copy-start
  370.9 12.4 %copy-start.1 = (bf16[64,32,512]{2,0,1:T(8,128)(2,1)S(1)}, bf16[64,32,512]{2,0,1:T(8,128)(2,1)}, u32[]{:S(2)}) copy-start(bf16[64,32,512]{2,0,1:T(8,128)(2,1)} %get-tuple-element.283) | copy-start | bytes 6291460 | tf_op jit(solution)/shard_map/while
  370.9 12.4 %copy-start.8 = (f32[32,64,512]{2,0,1:T(8,128)S(1)}, f32[32,64,512]{2,0,1:T(8,128)}, u32[]{:S(2)}) copy-start(f32[32,64,512]{2,0,1:T(8,128)} %fusion.861) | copy-start | bytes 12582916 | tf_op jit(solution)/shard_map/while
  383.3 10.7 %copy-start.4 = (f32[32,64,512]{2,0,1:T(8,128)S(1)}, f32[32,64,512]{2,0,1:T(8,128)}, u32[]{:S(2)}) copy-start(f32[32,64,512]{2,0,1:T(8,128)} %fusion.856) | copy-start | bytes 12582916 | tf_op jit(solution)/shard_map/while
  383.3 10.7 %copy-start.5 = (f32[32,64,512]{2,0,1:T(8,128)S(1)}, f32[32,64,512]{2,0,1:T(8,128)}, u32[]{:S(2)}) copy-start(f32[32,64,512]{2,0,1:T(8,128)} %fusion.857) | copy-start | bytes 12582916 | tf_op jit(solution)/shard_map/while
  383.3 10.7 %copy-start.6 = (f32[32,64,512]{2,0,1:T(8,128)S(1)}, f32[32,64,512]{2,0,1:T(8,128)}, u32[]{:S(2)}) copy-start(f32[32,64,512]{2,0,1:T(8,128)} %fusion.859) | copy-start | bytes 12582916 | tf_op jit(solution)/shard_map/while
  383.4 12.2 %copy-start.7 = (f32[32,64,512]{2,0,1:T(8,128)S(1)}, f32[32,64,512]{2,0,1:T(8,128)}, u32[]{:S(2)}) copy-start(f32[32,64,512]{2,0,1:T(8,128)} %fusion.860) | copy-start | bytes 12582916 | tf_op jit(solution)/shard_map/while
  423.8 163.3 %collective-permute-start = (bf16[1024,512]{1,0:T(8,128)(2,1)S(1)}, bf16[1024,512]{1,0:T(8,128)(2,1)}, u32[]{:S(2)}, u32[]{:S(2)}) collective-permute-start(bf16[1024,512]{1,0:T(8,128)(2,1)S(1)} %copy.404), channel_id=1, source_target_pairs={{0,8},{8,16},{16,24},{1,9},{9,17},{17,25},{2,10},{10,18},{18,26},{... | collective-permute-start | bytes 3145736 | tf_op jit(solution)/shard_map/while/body/eval_jaxpr/ppermute | solution.py:12
  520.6 3.9 copy-start.3
  524.5 3.7 copy-start.2
  528.2 3.7 copy-start
  535.7 12.4 %copy-start.1 = (bf16[64,32,512]{2,0,1:T(8,128)(2,1)S(1)}, bf16[64,32,512]{2,0,1:T(8,128)(2,1)}, u32[]{:S(2)}) copy-start(bf16[64,32,512]{2,0,1:T(8,128)(2,1)} %get-tuple-element.283) | copy-start | bytes 6291460 | tf_op jit(solution)/shard_map/while
  535.7 12.4 %copy-start.8 = (f32[32,64,512]{2,0,1:T(8,128)S(1)}, f32[32,64,512]{2,0,1:T(8,128)}, u32[]{:S(2)}) copy-start(f32[32,64,512]{2,0,1:T(8,128)} %fusion.861) | copy-start | bytes 12582916 | tf_op jit(solution)/shard_map/while
  548.1 10.7 %copy-start.4 = (f32[32,64,512]{2,0,1:T(8,128)S(1)}, f32[32,64,512]{2,0,1:T(8,128)}, u32[]{:S(2)}) copy-start(f32[32,64,512]{2,0,1:T(8,128)} %fusion.856) | copy-start | bytes 12582916 | tf_op jit(solution)/shard_map/while
  548.1 10.7 %copy-start.5 = (f32[32,64,512]{2,0,1:T(8,128)S(1)}, f32[32,64,512]{2,0,1:T(8,128)}, u32[]{:S(2)}) copy-start(f32[32,64,512]{2,0,1:T(8,128)} %fusion.857) | copy-start | bytes 12582916 | tf_op jit(solution)/shard_map/while
  548.1 10.7 %copy-start.6 = (f32[32,64,512]{2,0,1:T(8,128)S(1)}, f32[32,64,512]{2,0,1:T(8,128)}, u32[]{:S(2)}) copy-start(f32[32,64,512]{2,0,1:T(8,128)} %fusion.859) | copy-start | bytes 12582916 | tf_op jit(solution)/shard_map/while
  548.1 12.2 %copy-start.7 = (f32[32,64,512]{2,0,1:T(8,128)S(1)}, f32[32,64,512]{2,0,1:T(8,128)}, u32[]{:S(2)}) copy-start(f32[32,64,512]{2,0,1:T(8,128)} %fusion.860) | copy-start | bytes 12582916 | tf_op jit(solution)/shard_map/while
  618.5 5.0 copy-start.24
  618.5 5.0 copy-start.25
  705.0 3.7 copy-start.14
  708.7 3.7 copy-start.13
  708.7 7.5 copy-start.18
  712.4 3.7 copy-start.17
  725.4 11.7 %copy-start.15 = (f32[32,64,512]{2,0,1:T(8,128)S(1)}, f32[32,64,512]{2,0,1:T(8,128)}, u32[]{:S(2)}) copy-start(f32[32,64,512]{2,0,1:T(8,128)} %fusion.317) | copy-start | bytes 12582916
  725.4 11.7 %copy-start.16 = (f32[32,64,512]{2,0,1:T(8,128)S(1)}, f32[32,64,512]{2,0,1:T(8,128)}, u32[]{:S(2)}) copy-start(f32[32,64,512]{2,0,1:T(8,128)} %fusion.325) | copy-start | bytes 12582916
  763.5 6.4 copy-start.10
  769.9 3.4 copy-start.9
  860.6 3.9 copy-start.26
  864.5 3.5 copy-start.12
  864.5 3.5 copy-start.27
  (7 other events, 13.6 us)
Sparse Core Ops, SparseCore 0:
  881.9 88.9 reduce-scatter.1
